TPU v7x, 32 devices: a whole 2x2x4 slice. The times are simulated.
32 devices in a mesh: scene: 2 (over y), pts: 4 (over z), view: 2 (over x), head: 2 (over core).
Axes of the slice: x: 2, y: 2, z: 4, core: 2. Of those that a mesh axis runs over, the one named last changes fastest.
Arguments:
- queries: bfloat16 [2048, 1024], P(('scene', 'pts'), 'head'), parts along dimension 0, may hold values from -8 to 8
- key_tiles: bfloat16 [128, 16, 1024], P(('scene', 'pts', 'view'), None, 'head'), parts along dimension 0, may hold values from -4 to 4
- value_tiles: bfloat16 [128, 16, 1024], P(('scene', 'pts', 'view'), None, 'head'), parts along dimension 0, may hold values from -6 to 6
- visible: int32 [16, 32], P(('scene', 'pts'), 'view'), parts along dimension 0, may hold values from 0 to 63, as said below
- destination: int32 [2048], P(('scene', 'pts')), parts along dimension 0, may hold values from 0 to 1023, as said below
- d_out: bfloat16 [2048, 1024], P(('scene', 'pts'), 'head'), parts along dimension 0, may hold values from -6 to 6
Outputs:
- attended: bfloat16 [2048, 1024], P(('scene', 'pts'), 'head'), parts along dimension 0
- d_queries: bfloat16 [2048, 1024], P(('scene', 'pts'), 'head'), parts along dimension 0
- d_keys: bfloat16 [128, 16, 1024], P(('scene', 'pts', 'view'), None, 'head'), parts along dimension 0
- d_values: bfloat16 [128, 16, 1024], P(('scene', 'pts', 'view'), None, 'head'), parts along dimension 0
There are 2 independent parts, one for each index of `scene`. A program takes and returns all parts, laid end to end along the dimension named above; each array names one. Nothing has to cross between parts.
Inputs may be any that keep to these rules, and one draw needn't show every extreme that they name: `visible`: the 16 ids that one query block lists for view group v are distinct tiles held by devices of view index v. The lists of the query blocks of one pts index for one view group name exactly 32 distinct tiles, at most 8 of them held by any one device, and exactly 8 held by some device. `destination`: A permutation of the 1024 rows. The rows of each pts index go to the rows of every pts index, exactly 64 to each.
All inputs are finite; a program needn't handle non-finite values.
Results may differ from a plain program's by a relative error of at most 0.017.
Values may be sent and summed in bfloat16 or wider, within the bound.
A program may use at most 64 MiB of HBM per device.

v0:
```python
import math
import jax
import jax.numpy as jnp
from jax import lax
from jax.sharding import PartitionSpec as P

DH = 64
DIST = 32
HIGHEST = lax.Precision.HIGHEST


def merged(value, axis, join):
    pieces = jax.tree.map(lambda part: lax.all_gather(part, axis), value)
    head = jax.tree.map(lambda part: part[0], pieces)
    tail = jax.tree.map(lambda part: part[1:], pieces)
    running, _ = lax.scan(lambda running, share: (join(running, share), None), head, tail)
    return running


def fetch_tiles(requests, key_tiles, value_tiles):
    asked_ids = lax.all_to_all(requests, "pts", split_axis=0, concat_axis=0, tiled=True)
    safe_ids = jnp.maximum(asked_ids, 0)
    keys_out = jnp.take(key_tiles, safe_ids, axis=0)
    values_out = jnp.take(value_tiles, safe_ids, axis=0)
    keys_back = lax.all_to_all(keys_out, "pts", split_axis=0, concat_axis=0, tiled=True)
    values_back = lax.all_to_all(values_out, "pts", split_axis=0, concat_axis=0, tiled=True)
    return (keys_back, values_back, asked_ids)


def refetch_tiles(requests, key_tiles, value_tiles):
    safe_ids = jnp.maximum(
        lax.all_to_all(requests, "pts", split_axis=0, concat_axis=0, tiled=True), 0
    )
    keys_out = jnp.take(key_tiles, safe_ids, axis=0)
    values_out = jnp.take(value_tiles, safe_ids, axis=0)
    return (
        lax.all_to_all(keys_out, "pts", split_axis=0, concat_axis=0, tiled=True),
        lax.all_to_all(values_out, "pts", split_axis=0, concat_axis=0, tiled=True),
    )


def widen(stats):
    return jnp.repeat(stats, DH, axis=1)


def local(queries, key_tiles, value_tiles, visible, destination, d_out):
    pts_count = lax.axis_size("pts")
    view_count = lax.axis_size("view")
    kv_dev, tile_keys, local_width = key_tiles.shape
    qb_dev, nvis = visible.shape
    p_dev = queries.shape[0]
    qblock = p_dev // qb_dev
    heads_local = local_width // DH
    group_heads = math.gcd(heads_local, 4)
    group_width = group_heads * DH
    group_total = heads_local // group_heads
    capacity = max(2, min(kv_dev, 2 * DIST // pts_count))
    score_scale = DH ** (-0.5)
    slot_total = pts_count * capacity
    entries = visible.reshape(-1)
    entry_count = entries.shape[0]
    owner_of = entries // kv_dev // view_count
    local_id = entries % kv_dev
    positions = jnp.arange(entry_count)
    same_id = entries[:, None] == entries[None, :]
    earlier = positions[None, :] < positions[:, None]
    first_seen = jnp.logical_not(jnp.any(same_id & earlier, axis=1))
    same_owner = (owner_of[:, None] == owner_of[None, :]) & earlier & first_seen[None, :]
    owner_rank = jnp.sum(same_owner.astype(jnp.int32), axis=1)
    own_slot = owner_of * capacity + owner_rank
    slot_of = jnp.sum(jnp.where(same_id & first_seen[None, :], own_slot[None, :], 0), axis=1)
    slot_grid = jnp.arange(slot_total)
    slot_hit = (own_slot[None, :] == slot_grid[:, None]) & first_seen[None, :]
    requests = (jnp.sum(jnp.where(slot_hit, local_id[None, :] + 1, 0), axis=1) - 1).reshape(
        pts_count, capacity
    )
    slot_table = slot_of.reshape(qb_dev, nvis)

    def block_tiles(fetched):
        flat_tiles = fetched.reshape(slot_total, tile_keys, local_width)
        return jnp.take(flat_tiles, slot_table, axis=0).reshape(
            qb_dev, nvis * tile_keys, local_width
        )

    fetched_keys, fetched_values, asked = fetch_tiles(requests, key_tiles, value_tiles)
    block_keys = block_tiles(fetched_keys)
    block_values = block_tiles(fetched_values)
    query_blocks = queries.reshape(qb_dev, qblock, local_width)
    key_count = nvis * tile_keys
    peak_list, total_list, weighted_list = ([], [], [])
    for group_number in range(group_total):
        col_start = group_number * group_width
        col_stop = col_start + group_width
        query_part = query_blocks[..., col_start:col_stop].reshape(qb_dev, qblock, group_heads, DH)
        key_part = block_keys[..., col_start:col_stop].reshape(qb_dev, key_count, group_heads, DH)
        value_part = block_values[..., col_start:col_stop].reshape(
            qb_dev, key_count, group_heads, DH
        )
        scores = (
            jnp.einsum("bqhd,bkhd->bhqk", query_part, key_part, preferred_element_type=jnp.float32)
            * score_scale
        )
        local_peak = jnp.max(scores, axis=-1)
        exponent = jnp.exp(scores - local_peak[..., None])
        local_total = jnp.sum(exponent, axis=-1)
        weighted = jnp.einsum(
            "bhqk,bkhd->bqhd",
            exponent.astype(jnp.bfloat16),
            value_part,
            preferred_element_type=jnp.float32,
        )
        peak_list.append(jnp.transpose(local_peak, (0, 2, 1)))
        total_list.append(jnp.transpose(local_total, (0, 2, 1)))
        weighted_list.append(weighted.reshape(qb_dev, qblock, group_width))
    peak_rows = jnp.concatenate(peak_list, axis=-1).reshape(p_dev, heads_local)
    total_rows = jnp.concatenate(total_list, axis=-1).reshape(p_dev, heads_local)
    weighted_rows = jnp.concatenate(weighted_list, axis=-1).reshape(p_dev, local_width)

    def join(first_part, second_part):
        peak_a, total_a, sum_a = first_part
        peak_b, total_b, sum_b = second_part
        peak_top = jnp.maximum(peak_a, peak_b)
        factor_a = jnp.exp(peak_a - peak_top)
        factor_b = jnp.exp(peak_b - peak_top)
        return (
            peak_top,
            factor_a * total_a + factor_b * total_b,
            widen(factor_a) * sum_a + widen(factor_b) * sum_b,
        )

    big_peak, big_total, big_sum = merged((peak_rows, total_rows, weighted_rows), "view", join)
    attended_rows = (big_sum / widen(big_total)).astype(jnp.bfloat16)
    again_keys, again_values = refetch_tiles(requests, key_tiles, value_tiles)
    grad_keys = block_tiles(again_keys)
    grad_values = block_tiles(again_values)
    delta_rows = jnp.sum(
        (d_out.astype(jnp.float32) * attended_rows.astype(jnp.float32)).reshape(
            p_dev, heads_local, DH
        ),
        axis=-1,
    )
    peak_heads = big_peak.reshape(qb_dev, qblock, heads_local)
    total_heads = big_total.reshape(qb_dev, qblock, heads_local)
    delta_heads = delta_rows.reshape(qb_dev, qblock, heads_local)
    grad_blocks = d_out.reshape(qb_dev, qblock, local_width)
    dquery_list, dkey_list, dvalue_list = ([], [], [])
    for group_number in range(group_total):
        col_start = group_number * group_width
        col_stop = col_start + group_width
        head_start = group_number * group_heads
        head_stop = head_start + group_heads
        query_part = query_blocks[..., col_start:col_stop].reshape(qb_dev, qblock, group_heads, DH)
        key_part = grad_keys[..., col_start:col_stop].reshape(qb_dev, key_count, group_heads, DH)
        value_part = grad_values[..., col_start:col_stop].reshape(
            qb_dev, key_count, group_heads, DH
        )
        grad_part = grad_blocks[..., col_start:col_stop].reshape(qb_dev, qblock, group_heads, DH)
        peak_part = jnp.transpose(peak_heads[..., head_start:head_stop], (0, 2, 1))[..., None]
        total_part = jnp.transpose(total_heads[..., head_start:head_stop], (0, 2, 1))[..., None]
        delta_part = jnp.transpose(delta_heads[..., head_start:head_stop], (0, 2, 1))[..., None]
        scores = (
            jnp.einsum("bqhd,bkhd->bhqk", query_part, key_part, preferred_element_type=jnp.float32)
            * score_scale
        )
        probability = jnp.exp(scores - peak_part) / total_part
        value_grad = jnp.einsum(
            "bhqk,bqhd->bkhd",
            probability.astype(jnp.bfloat16),
            grad_part,
            preferred_element_type=jnp.float32,
        )
        d_prob = jnp.einsum(
            "bqhd,bkhd->bhqk", grad_part, value_part, preferred_element_type=jnp.float32
        )
        d_score = (probability * (d_prob - delta_part)).astype(jnp.bfloat16)
        query_grad = (
            jnp.einsum("bhqk,bkhd->bqhd", d_score, key_part, preferred_element_type=jnp.float32)
            * score_scale
        )
        key_grad = (
            jnp.einsum("bhqk,bqhd->bkhd", d_score, query_part, preferred_element_type=jnp.float32)
            * score_scale
        )
        dquery_list.append(query_grad.reshape(qb_dev, qblock, group_width))
        dkey_list.append(key_grad.reshape(qb_dev, key_count, group_width))
        dvalue_list.append(value_grad.reshape(qb_dev, key_count, group_width))
    dquery_local = jnp.concatenate(dquery_list, axis=-1).reshape(p_dev, local_width)
    dkey_blocks = jnp.concatenate(dkey_list, axis=-1)
    dvalue_blocks = jnp.concatenate(dvalue_list, axis=-1)
    d_queries = lax.psum(dquery_local, "view").astype(jnp.bfloat16)
    slot_match = (slot_of[None, :] == slot_grid[:, None]).astype(jnp.float32)

    def per_slot(blocks):
        flat_rows = blocks.reshape(qb_dev * nvis, tile_keys * local_width)
        summed = jnp.dot(
            slot_match, flat_rows, precision=HIGHEST, preferred_element_type=jnp.float32
        )
        return summed.astype(jnp.bfloat16).reshape(pts_count, capacity, tile_keys, local_width)

    back_keys, back_values = (
        lax.all_to_all(per_slot(dkey_blocks), "pts", split_axis=0, concat_axis=0, tiled=True),
        lax.all_to_all(per_slot(dvalue_blocks), "pts", split_axis=0, concat_axis=0, tiled=True),
    )
    owner_match = (asked.reshape(-1)[None, :] == jnp.arange(kv_dev)[:, None]).astype(jnp.bfloat16)
    d_keys = (
        jnp.dot(
            owner_match,
            back_keys.reshape(slot_total, tile_keys * local_width),
            preferred_element_type=jnp.float32,
        )
        .astype(jnp.bfloat16)
        .reshape(kv_dev, tile_keys, local_width)
    )
    d_values = (
        jnp.dot(
            owner_match,
            back_values.reshape(slot_total, tile_keys * local_width),
            preferred_element_type=jnp.float32,
        )
        .astype(jnp.bfloat16)
        .reshape(kv_dev, tile_keys, local_width)
    )
    per_peer = p_dev // pts_count
    target = destination // p_dev
    row_place = destination % p_dev
    peer_hits = (target[:, None] == jnp.arange(pts_count)[None, :]).astype(jnp.int32)
    before = jnp.cumsum(peer_hits, axis=0) - peer_hits
    send_rank = jnp.sum(before * peer_hits, axis=1)
    send_position = target * per_peer + send_rank
    row_numbers = jnp.arange(p_dev, dtype=jnp.int32)
    send_inverse = jnp.zeros((p_dev,), jnp.int32).at[send_position].set(row_numbers)
    rows_out = attended_rows[send_inverse].reshape(pts_count, per_peer, local_width)
    places_out = row_place[send_inverse].reshape(pts_count, per_peer)
    got_rows, got_places = (
        lax.all_to_all(rows_out, "pts", split_axis=0, concat_axis=0, tiled=True),
        lax.all_to_all(places_out, "pts", split_axis=0, concat_axis=0, tiled=True),
    )
    place_inverse = jnp.zeros((p_dev,), jnp.int32).at[got_places.reshape(-1)].set(row_numbers)
    attended = got_rows.reshape(p_dev, local_width)[place_inverse]
    return (attended, d_queries, d_keys, d_values)


def solution(mesh):
    in_specs = (
        P(("scene", "pts"), "head"),
        P(("scene", "pts", "view"), None, "head"),
        P(("scene", "pts", "view"), None, "head"),
        P(("scene", "pts"), "view"),
        P(("scene", "pts")),
        P(("scene", "pts"), "head"),
    )
    out_specs = (
        P(("scene", "pts"), "head"),
        P(("scene", "pts"), "head"),
        P(("scene", "pts", "view"), None, "head"),
        P(("scene", "pts", "view"), None, "head"),
    )
    return jax.shard_map(local, mesh=mesh, in_specs=in_specs, out_specs=out_specs, check_vma=False)
```

profile of v0, /device:TPU:0, one launch (start us, length us, event | category | flops | bytes accessed | tf_op | source)
XLA Modules:
  0.0 160.3 jit_solution(14383902787130595014)
XLA Ops:
  7.2 0.8 reshape.364
  9.2 6.4 %all-to-all-start = ((s32[4,1,8]{2,1,0:T(1,128)}), s32[4,1,8]{2,1,0:T(1,128)S(1)}, u32[]{:S(2)}, u32[]{:S(2)}) async-start(s32[4,1,8]{2,1,0:T(1,128)} %bitcast), calls=%async_computation | async-start | bytes 4096 | tf_op jit(solution)/shard_map/all_to_all | solution.py:21
  15.7 1.2 reduce-window.6
  17.4 3.7 %all-to-all-done = s32[4,1,8]{2,1,0:T(1,128)S(1)} async-done(((s32[4,1,8]{2,1,0:T(1,128)}), s32[4,1,8]{2,1,0:T(1,128)S(1)}, u32[]{:S(2)}, u32[]{:S(2)}) %all-to-all-start) | async-done | bytes 160 | tf_op jit(solution)/shard_map/all_to_all | solution.py:21
  21.7 1.2 fusion.56
  24.5 1.2 broadcast_select_fusion.2
  25.7 3.6 %all-to-all-start.2 = ((bf16[4,8,16,512]{3,2,1,0:T(8,128)(2,1)}), bf16[4,8,16,512]{3,2,1,0:T(8,128)(2,1)S(1)}, u32[]{:S(2)}, u32[]{:S(2)}) async-start(bf16[4,8,16,512]{3,2,1,0:T(8,128)(2,1)} %get-tuple-element.72), calls=%async_computation.2 | async-start | bytes 1048576 | tf_op jit(solution)/shard_map/all_to_all | solution.py:26
  29.4 1.4 scatter_custom_fusion
  30.8 11.8 %all-to-all-done.2 = bf16[4,8,16,512]{3,2,1,0:T(8,128)(2,1)S(1)} async-done(((bf16[4,8,16,512]{3,2,1,0:T(8,128)(2,1)}), bf16[4,8,16,512]{3,2,1,0:T(8,128)(2,1)S(1)}, u32[]{:S(2)}, u32[]{:S(2)}) %all-to-all-start.2) | async-done | bytes 524320 | tf_op jit(solution)/shard_map/all_to_all | solution.py:26
  42.6 3.5 %all-to-all-start.1 = ((bf16[4,8,16,512]{3,2,1,0:T(8,128)(2,1)}), bf16[4,8,16,512]{3,2,1,0:T(8,128)(2,1)S(1)}, u32[]{:S(2)}, u32[]{:S(2)}) async-start(bf16[4,8,16,512]{3,2,1,0:T(8,128)(2,1)} %get-tuple-element.73), calls=%async_computation.1 | async-start | bytes 1048576 | tf_op jit(solution)/shard_map/all_to_all | solution.py:25
  46.5 1.9 %gather_fusion.1 = s32[256]{0:T(256)S(1)} fusion(s32[256]{0:T(256)S(1)} %get-tuple-element.68, s32[1024]{0:T(1024)S(1)} %pad_clamp_fusion.1), kind=kCustom, calls=%fused_computation.5 | custom fusion | bytes 3072 | tf_op jit(solution)/shard_map/gather | solution.py:233
  49.2 0.8 copy.142
  49.9 0.8 copy.141
  51.3 8.6 %all-to-all-done.1 = bf16[4,8,16,512]{3,2,1,0:T(8,128)(2,1)S(1)} async-done(((bf16[4,8,16,512]{3,2,1,0:T(8,128)(2,1)}), bf16[4,8,16,512]{3,2,1,0:T(8,128)(2,1)S(1)}, u32[]{:S(2)}, u32[]{:S(2)}) %all-to-all-start.1) | async-done | bytes 524320 | tf_op jit(solution)/shard_map/all_to_all | solution.py:25
  59.9 3.8 %all-to-all-start.4 = ((s32[4,1,64]{2,1,0:T(1,128)}), s32[4,1,64]{2,1,0:T(1,128)}, u32[]{:S(2)}, u32[]{:S(2)}) async-start(s32[4,1,64]{2,1,0:T(1,128)} %all_to_all.32), calls=%async_computation.4 | async-start | bytes 4096 | tf_op jit(solution)/shard_map/all_to_all | solution.py:236
  66.5 4.4 %all_gather.11 = f32[2,256,8]{1,2,0:T(8,128)S(1)} all-gather(f32[1,256,8]{1,2,0:T(8,128)S(1)} %maximum_bitcast_fusion.1), channel_id=1, replica_groups=mesh['scene'=2,'pts'=4,'view'=2,'head'=2] {'view'}, dimensions={0}, use_global_device_ids=true | all-gather | bytes 24576 | tf_op jit(solution)/shard_map/all_gather | solution.py:13
  70.9 4.5 %all_gather.9 = f32[2,256,8]{1,2,0:T(8,128)} all-gather(f32[1,256,8]{1,2,0:T(8,128)S(1)} %maximum_bitcast_fusion), channel_id=1, replica_groups=mesh['scene'=2,'pts'=4,'view'=2,'head'=2] {'view'}, dimensions={0}, use_global_device_ids=true | all-gather | bytes 24576 | tf_op jit(solution)/shard_map/all_gather | solution.py:13
  76.2 1.0 convolution_bitcast_fusion
  78.5 1.0 convolution_bitcast_fusion.1
  79.9 1.0 copy.107
  82.3 1.0 copy.127
  83.6 1.0 copy.126
  84.6 1.3 pad_maximum_fusion.1
  85.9 1.2 reshape.397
  87.1 2.7 %convolution_convert_fusion = bf16[32,8192]{1,0:T(8,128)(2,1)} fusion(f32[32,8192]{1,0:T(8,128)} %reshape.397, s32[32]{0:T(128)} %copy-done.27), kind=kOutput, calls=%fused_computation.9 | convolution fusion | flops 100926464 | bytes 1572992 | tf_op jit(solution)/shard_map/dot_general | solution.py:195
  89.8 5.1 %all-to-all-start.6 = ((bf16[4,8,16,512]{3,1,2,0:T(8,128)(2,1)}), bf16[4,8,16,512]{3,1,2,0:T(8,128)(2,1)S(1)}, u32[]{:S(2)}, u32[]{:S(2)}) async-start(bf16[4,8,16,512]{3,1,2,0:T(8,128)(2,1)} %bitcast.72), calls=%async_computation.6 | async-start | bytes 1048576 | tf_op jit(solution)/shard_map/all_to_all | solution.py:202
  95.6 1.3 reduce.6
  97.0 1.6 scatter_custom_fusion.1
  99.8 0.8 broadcast_in_dim.84
  100.6 1.2 copy.110
  101.9 0.8 broadcast_in_dim.53
  102.7 2.0 %copy.109 = f32[256,512]{1,0:T(8,128)} copy(f32[256,512]{0,1:T(8,128)} %bitcast.232) | data formatting | bytes 1048576 | tf_op jit(solution)/shard_map/while/body/eval_jaxpr/reshape | solution.py:43
  104.8 0.8 broadcast_in_dim.52
  105.6 2.0 %copy.108 = f32[256,512]{1,0:T(8,128)} copy(f32[256,512]{0,1:T(8,128)} %bitcast.233) | data formatting | bytes 1048576 | tf_op jit(solution)/shard_map/while/body/eval_jaxpr/reshape | solution.py:43
  108.5 0.7 copy.130
  109.5 2.6 %convert_multiply_fusion = (f32[256,512]{1,0:T(8,128)}, bf16[256,512]{1,0:T(8,128)(2,1)S(1)}) fusion(bf16[256,512]{1,0:T(8,128)(2,1)S(1)} %copy-done.9, f32[256,512]{1,0:T(8,128)S(1)} %copy.110, f32[256,512]{1,0:T(8,128)} %copy.109, f32[2,256,512]{2,1,0:T(8,128)} %all-gather.2.cloned.1.call-done, f32[256,512]{1,0:T(8,128)} %copy.108), kind=kLoop, calls=%fused_computation.56 | loop fusion | flops 1048576 | bytes 3670016 | tf_op jit(solution)/shard_map/mul | solution.py:137
  112.1 1.2 copy.114
  113.5 0.8 copy-done.13
  116.5 2.0 %gather_fusion = bf16[256,512]{1,0:T(8,128)(2,1)} fusion(bf16[256,512]{1,0:T(8,128)(2,1)S(1)} %get-tuple-element.48, s32[1024]{0:T(1024)} %copy-done.25), kind=kCustom, calls=%fused_computation.4 | custom fusion | bytes 525312 | tf_op jit(solution)/shard_map/gather | solution.py:232
  118.5 5.1 %all-to-all-start.3 = ((bf16[4,64,512]{2,1,0:T(8,128)(2,1)}), bf16[4,64,512]{2,1,0:T(8,128)(2,1)S(1)}, u32[]{:S(2)}, u32[]{:S(2)}) async-start(bf16[4,64,512]{2,1,0:T(8,128)(2,1)} %bitcast.39), calls=%async_computation.3 | async-start | bytes 524288 | tf_op jit(solution)/shard_map/all_to_all | solution.py:235
  123.9 0.9 copy-done.11
  127.5 1.4 convolution_convert_fusion.1
  128.9 1.5 all-to-all-done.3
  130.4 3.6 %all-to-all-start.5 = ((bf16[4,8,16,512]{3,1,2,0:T(8,128)(2,1)}), bf16[4,8,16,512]{3,1,2,0:T(8,128)(2,1)S(1)}, u32[]{:S(2)}, u32[]{:S(2)}) async-start(bf16[4,8,16,512]{3,1,2,0:T(8,128)(2,1)} %bitcast.65), calls=%async_computation.5 | async-start | bytes 1048576 | tf_op jit(solution)/shard_map/all_to_all | solution.py:201
  134.5 15.3 %all-reduce.1 = bf16[256,512]{0,1:T(8,128)(2,1)S(1)} all-reduce(f32[256,512]{0,1:T(8,128)S(1)} %pad_maximum_fusion.3), channel_id=1, replica_groups=mesh['scene'=2,'pts'=4,'view'=2,'head'=2] {'view'}, use_global_device_ids=true, to_apply=%region_14.17 | all-reduce | flops 131072 | bytes 786432 | tf_op jit(solution)/shard_map/psum | solution.py:190
  149.8 0.8 copy.128
  150.6 2.0 %gather_fusion.2 = bf16[256,512]{1,0:T(8,128)(2,1)} fusion(bf16[256,512]{1,0:T(8,128)(2,1)S(1)} %bitcast.215, s32[1024]{0:T(1024)} %pad_clamp_fusion), kind=kCustom, calls=%fused_computation.6 | custom fusion | bytes 525312 | tf_op jit(solution)/shard_map/gather | solution.py:239
  152.8 0.7 copy.129
  (170 shorter events, 21.3 us)
Async XLA Ops:
  7.2 15.9 %copy-start = (bf16[8,16,512]{2,1,0:T(8,128)(2,1)S(1)}, bf16[8,16,512]{2,1,0:T(8,128)(2,1)}, u32[]{:S(2)}) copy-start(bf16[8,16,512]{2,1,0:T(8,128)(2,1)} %param.12) | copy-start | bytes 393220
  8.6 8.8 %copy-start.27 = (s32[32]{0:T(128)}, s32[32]{0:T(128)S(1)}, u32[]{:S(2)}) copy-start(s32[32]{0:T(128)S(1)} %get-tuple-element.43) | copy-start | bytes 388
  9.2 6.5 %copy-start.38 = (s32[256]{0:T(256)S(1)}, s32[256]{0:T(256)}, u32[]{:S(2)}) copy-start(s32[256]{0:T(256)} %param.14) | copy-start | bytes 3076
  9.2 11.9 %all-to-all-start = ((s32[4,1,8]{2,1,0:T(1,128)}), s32[4,1,8]{2,1,0:T(1,128)S(1)}, u32[]{:S(2)}, u32[]{:S(2)}) async-start(s32[4,1,8]{2,1,0:T(1,128)} %bitcast), calls=%async_computation | async-start | bytes 4096 | tf_op jit(solution)/shard_map/all_to_all | solution.py:21
  23.1 0.9 copy-start.3
  25.7 5.1 %copy-start.14 = (bf16[256,512]{1,0:T(8,128)(2,1)S(1)}, bf16[256,512]{1,0:T(8,128)(2,1)}, u32[]{:S(2)}) copy-start(bf16[256,512]{1,0:T(8,128)(2,1)} %param.10) | copy-start | bytes 786436
  25.7 16.9 %all-to-all-start.2 = ((bf16[4,8,16,512]{3,2,1,0:T(8,128)(2,1)}), bf16[4,8,16,512]{3,2,1,0:T(8,128)(2,1)S(1)}, u32[]{:S(2)}, u32[]{:S(2)}) async-start(bf16[4,8,16,512]{3,2,1,0:T(8,128)(2,1)} %get-tuple-element.72), calls=%async_computation.2 | async-start | bytes 1048576 | tf_op jit(solution)/shard_map/all_to_all | solution.py:26
  42.6 17.3 %all-to-all-start.1 = ((bf16[4,8,16,512]{3,2,1,0:T(8,128)(2,1)}), bf16[4,8,16,512]{3,2,1,0:T(8,128)(2,1)S(1)}, u32[]{:S(2)}, u32[]{:S(2)}) async-start(bf16[4,8,16,512]{3,2,1,0:T(8,128)(2,1)} %get-tuple-element.73), calls=%async_computation.1 | async-start | bytes 1048576 | tf_op jit(solution)/shard_map/all_to_all | solution.py:25
  46.3 18.5 %copy-start.6 = (bf16[2,128,256]{1,2,0:T(8,128)(2,1)}, bf16[2,128,256]{1,2,0:T(8,128)(2,1)S(1)}, u32[]{:S(2)}) copy-start(bf16[2,128,256]{1,2,0:T(8,128)(2,1)S(1)} %copy.140) | copy-start | bytes 393220
  46.5 19.4 %copy-start.4 = (bf16[2,128,256]{1,2,0:T(8,128)(2,1)}, bf16[2,128,256]{1,2,0:T(8,128)(2,1)S(1)}, u32[]{:S(2)}) copy-start(bf16[2,128,256]{1,2,0:T(8,128)(2,1)S(1)} %copy.139) | copy-start | bytes 393220
  46.5 2.0 %copy-start.25 = (s32[1024]{0:T(1024)}, s32[1024]{0:T(1024)S(1)}, u32[]{:S(2)}) copy-start(s32[1024]{0:T(1024)S(1)} %pad_clamp_fusion.1) | copy-start | bytes 12292
  46.5 2.6 %copy-start.8 = (bf16[256,512]{1,0:T(8,128)(2,1)S(1)}, bf16[256,512]{1,0:T(8,128)(2,1)}, u32[]{:S(2)}) copy-start(bf16[256,512]{1,0:T(8,128)(2,1)} %param.15) | copy-start | bytes 786436
  59.9 29.9 %all-to-all-start.4 = ((s32[4,1,64]{2,1,0:T(1,128)}), s32[4,1,64]{2,1,0:T(1,128)}, u32[]{:S(2)}, u32[]{:S(2)}) async-start(s32[4,1,64]{2,1,0:T(1,128)} %all_to_all.32), calls=%async_computation.4 | async-start | bytes 4096 | tf_op jit(solution)/shard_map/all_to_all | solution.py:236
  63.7 45.6 %all-gather.2.cloned.1.call-start = ((), (), s32[]{:S(2)}) async-start(), calls=%async_computation.7 | async-start | bytes 1572864 | tf_op jit(solution)/shard_map/all_gather | solution.py:13
  64.7 0.7 copy-start.1
  65.7 5.1 %copy-start.22 = (f32[2,4,128]{2,1,0:T(4,128)}, f32[2,4,128]{2,1,0:T(4,128)S(1)}, u32[]{:S(2)}) copy-start(f32[2,4,128]{2,1,0:T(4,128)S(1)} %get-tuple-element.76) | copy-start | bytes 12292
  66.3 4.6 %copy-start.21 = (f32[2,4,128]{2,1,0:T(4,128)}, f32[2,4,128]{2,1,0:T(4,128)S(1)}, u32[]{:S(2)}) copy-start(f32[2,4,128]{2,1,0:T(4,128)S(1)} %get-tuple-element.78) | copy-start | bytes 12292
  75.5 0.7 copy-start.12
  77.8 0.7 copy-start.10
  80.9 0.7 copy-start.15
  80.9 0.9 copy-start.19
  81.7 0.6 copy-start.34
  81.7 0.6 copy-start.36
  81.7 1.6 copy-start.30
  81.7 1.6 copy-start.32
  82.3 1.0 copy-start.17
  89.8 5.1 %copy-start.26 = (s32[4,8]{1,0:T(4,128)S(1)}, s32[4,8]{1,0:T(4,128)}, u32[]{:S(2)}) copy-start(s32[4,8]{1,0:T(4,128)} %get-tuple-element.66) | copy-start | bytes 388
  89.8 17.9 %all-to-all-start.6 = ((bf16[4,8,16,512]{3,1,2,0:T(8,128)(2,1)}), bf16[4,8,16,512]{3,1,2,0:T(8,128)(2,1)S(1)}, u32[]{:S(2)}, u32[]{:S(2)}) async-start(bf16[4,8,16,512]{3,1,2,0:T(8,128)(2,1)} %bitcast.72), calls=%async_computation.6 | async-start | bytes 1048576 | tf_op jit(solution)/shard_map/all_to_all | solution.py:202
  94.9 4.3 %copy-start.16 = (f32[2,256,8]{1,2,0:T(8,128)S(1)}, f32[2,256,8]{1,2,0:T(8,128)}, u32[]{:S(2)}) copy-start(f32[2,256,8]{1,2,0:T(8,128)} %all_gather.9) | copy-start | bytes 49156
  100.6 1.3 copy-start.24
  102.7 2.0 %copy-start.23 = (f32[256,8]{0,1:T(8,128)S(1)}, f32[256,8]{0,1:T(8,128)}, u32[]{:S(2)}) copy-start(f32[256,8]{0,1:T(8,128)} %get-tuple-element.50) | copy-start | bytes 24580
  107.7 0.7 copy-start.29
  108.5 1.0 copy-start.9
  113.4 1.0 copy-start.13
  113.4 1.0 copy-start.20
  113.4 0.9 copy-start.35
  113.5 0.9 copy-start.37
  114.4 1.0 copy-start.2
  115.3 0.9 copy-start.7
  118.5 11.9 %all-to-all-start.3 = ((bf16[4,64,512]{2,1,0:T(8,128)(2,1)}), bf16[4,64,512]{2,1,0:T(8,128)(2,1)S(1)}, u32[]{:S(2)}, u32[]{:S(2)}) async-start(bf16[4,64,512]{2,1,0:T(8,128)(2,1)} %bitcast.39), calls=%async_computation.3 | async-start | bytes 524288 | tf_op jit(solution)/shard_map/all_to_all | solution.py:235
  123.8 1.0 copy-start.11
  123.8 1.0 copy-start.18
  123.8 1.0 copy-start.31
  123.8 1.0 copy-start.33
  125.2 0.9 copy-start.5
  126.8 0.7 copy-start.28
  130.4 22.2 %all-to-all-start.5 = ((bf16[4,8,16,512]{3,1,2,0:T(8,128)(2,1)}), bf16[4,8,16,512]{3,1,2,0:T(8,128)(2,1)S(1)}, u32[]{:S(2)}, u32[]{:S(2)}) async-start(bf16[4,8,16,512]{3,1,2,0:T(8,128)(2,1)} %bitcast.65), calls=%async_computation.5 | async-start | bytes 1048576 | tf_op jit(solution)/shard_map/all_to_all | solution.py:201
Sparse Core Ops, SparseCore 0:
  81.1 22.6 all-gather.1
where the time goes:
time: 161 us; the launch traced here: 160 us
  local copies, waits for them, and re-layouts  43.3 us (27%)
  starting transfers between devices  31.1 us (19%)
  waiting for transfers between devices  25.7 us (16%)
  blocking collectives  24.1 us (15%)
  between operations  14.8 us (9%)
  other arithmetic  11.7 us (7%)
  matrix products  9.66 us (6%)
    psum x1, blocking collectives, local(): d_queries = lax.psum(dquery_local, 'view').astype(jnp.bfloat16)  15.3 us
    unnamed x87, local copies, waits for them, and re-layouts  12.4 us
    all_to_all x1, waiting for transfers between devices, fetch_tiles(): lax.all_to_all(values_out, 'pts', split_axis=0, concat_axis=0, tiled=True)  11.8 us
    all_gather x2, blocking collectives, merged(): pieces = jax.tree.map(lambda part: lax.all_gather(part, axis), value)  8.84 us
    all_to_all x1, waiting for transfers between devices, fetch_tiles(): lax.all_to_all(keys_out, 'pts', split_axis=0, concat_axis=0, tiled=True)  8.62 us
    all_to_all x1, starting transfers between devices, fetch_tiles(): lax.all_to_all(requests, 'pts', split_axis=0, concat_axis=0, tiled=True)  6.45 us
    reshape x3, local copies, waits for them, and re-layouts, widen(): return jnp.repeat(stats, DH, axis=1)  5.34 us
    all_to_all x1, starting transfers between devices, local(): lax.all_to_all(per_slot(dvalue_blocks), 'pts', split_axis=0, concat_axis=...  5.14 us
  transfers between devices with their start and end apart: 8, of which 4 were waited for; matrix products, arithmetic and copies ran while one was open for 26% of the time, Pallas kernels for 0%

commit v1 on v0

--- a/solution.py
+++ b/solution.py
@@ -7,6 +7,28 @@
 DH = 64
 DIST = 32
 HIGHEST = lax.Precision.HIGHEST
+
+
+def cut_along(x, dim, devices):
+    before, after = (x.shape[:dim], x.shape[dim + 1 :])
+    return jnp.moveaxis(x.reshape(*before, devices, -1, *after), dim, 0)
+
+
+def in_order(tiles, dim):
+    tiles = jnp.moveaxis(tiles, 0, dim)
+    shape = tiles.shape
+    return tiles.reshape(*shape[:dim], shape[dim] * shape[dim + 1], *shape[dim + 2 :])
+
+
+def exchange_in_pairs(array, axis, split_dim, concat_dim):
+    devices, index = (lax.axis_size(axis), lax.axis_index(axis))
+    blocks = cut_along(array, split_dim, devices)
+    gathered = [blocks[index]]
+    for turn in range(1, devices):
+        sent = blocks[index ^ turn]
+        gathered.append(lax.ppermute(sent, axis, [(i, i ^ turn) for i in range(devices)]))
+    blocks = jnp.stack(gathered)[index ^ jnp.arange(devices)]
+    return in_order(blocks, concat_dim)
 
 
 def merged(value, axis, join):
@@ -233,7 +255,7 @@
     places_out = row_place[send_inverse].reshape(pts_count, per_peer)
     got_rows, got_places = (
         lax.all_to_all(rows_out, "pts", split_axis=0, concat_axis=0, tiled=True),
-        lax.all_to_all(places_out, "pts", split_axis=0, concat_axis=0, tiled=True),
+        exchange_in_pairs(places_out, "pts", 0, 0),
     )
     place_inverse = jnp.zeros((p_dev,), jnp.int32).at[got_places.reshape(-1)].set(row_numbers)
     attended = got_rows.reshape(p_dev, local_width)[place_inverse]

time: 161 us -> 156 us (0.969)
  waiting for transfers between devices: 25.7 us -> 20.1 us
    all_to_all x1, waiting for transfers between devices: 11.8 us -> 5.77 us  [fetch_tiles(): lax.all_to_all(values_out, 'pts', split_axis=0, concat_axis=0, tiled=True)]
    ppermute x0 -> x3, starting transfers between devices: none -> 4.39 us  [exchange_in_pairs(): lax.ppermute(sent, axis, [(i, i ^ turn) for i in range(devices)])]
    all_to_all x1 -> x0, starting transfers between devices: 3.76 us -> none  [local(): lax.all_to_all(places_out, 'pts', split_axis=0, concat_axis=0, tiled=True)]
    all_to_all x1, waiting for transfers between devices: 8.62 us -> 10.3 us  [fetch_tiles(): lax.all_to_all(keys_out, 'pts', split_axis=0, concat_axis=0, tiled=True)]
    all_to_all x1, starting transfers between devices: 5.14 us -> 3.47 us  [local(): lax.all_to_all(per_slot(dvalue_blocks), 'pts', split_axis=0, concat_axis=...]
  transfers between devices with their start and end apart: 8 -> 10, of which waited for: 4 -> 4; matrix products, arithmetic and copies ran while one was open for 26% -> 28% of each run, Pallas kernels for 0% -> 0%
where the time goes in v1:
time: 156 us; the launch traced here: 155 us
  local copies, waits for them, and re-layouts  44.7 us (29%)
  starting transfers between devices  30 us (19%)
  blocking collectives  24.7 us (16%)
  waiting for transfers between devices  20.1 us (13%)
  between operations  14.9 us (10%)
  other arithmetic  11.1 us (7%)
  matrix products  9.64 us (6%)
    psum x1, blocking collectives, local(): d_queries = lax.psum(dquery_local, 'view').astype(jnp.bfloat16)  15.9 us
    unnamed x87, local copies, waits for them, and re-layouts  13 us
    all_to_all x1, waiting for transfers between devices, fetch_tiles(): lax.all_to_all(keys_out, 'pts', split_axis=0, concat_axis=0, tiled=True)  10.3 us
    all_gather x2, blocking collectives, merged(): pieces = jax.tree.map(lambda part: lax.all_gather(part, axis), value)  8.84 us
    all_to_all x1, starting transfers between devices, fetch_tiles(): lax.all_to_all(requests, 'pts', split_axis=0, concat_axis=0, tiled=True)  6.45 us
    all_to_all x1, waiting for transfers between devices, fetch_tiles(): lax.all_to_all(values_out, 'pts', split_axis=0, concat_axis=0, tiled=True)  5.77 us
    reshape x3, local copies, waits for them, and re-layouts, widen(): return jnp.repeat(stats, DH, axis=1)  5.35 us
    all_to_all x1, starting transfers between devices, local(): lax.all_to_all(rows_out, 'pts', split_axis=0, concat_axis=0, tiled=True)  5.04 us
  transfers between devices with their start and end apart: 10, of which 4 were waited for; matrix products, arithmetic and copies ran while one was open for 28% of the time, Pallas kernels for 0%

profile of v1, /device:TPU:0, one launch (start us, length us, event | category | flops | bytes accessed | tf_op | source)
XLA Modules:
  0.0 155.0 jit_solution(2837900586629046760)
XLA Ops:
  7.2 0.8 reshape.372
  9.2 6.4 %all-to-all-start = ((s32[4,1,8]{2,1,0:T(1,128)}), s32[4,1,8]{2,1,0:T(1,128)S(1)}, u32[]{:S(2)}, u32[]{:S(2)}) async-start(s32[4,1,8]{2,1,0:T(1,128)} %bitcast), calls=%async_computation | async-start | bytes 4096 | tf_op jit(solution)/shard_map/all_to_all | solution.py:43
  15.7 1.2 reduce-window.6
  17.4 1.4 scatter_custom_fusion
  18.8 2.4 %all-to-all-done = s32[4,1,8]{2,1,0:T(1,128)S(1)} async-done(((s32[4,1,8]{2,1,0:T(1,128)}), s32[4,1,8]{2,1,0:T(1,128)S(1)}, u32[]{:S(2)}, u32[]{:S(2)}) %all-to-all-start) | async-done | bytes 160 | tf_op jit(solution)/shard_map/all_to_all | solution.py:43
  24.0 1.2 broadcast_select_fusion.2
  25.1 3.5 %all-to-all-start.2 = ((bf16[4,8,16,512]{3,2,1,0:T(8,128)(2,1)}), bf16[4,8,16,512]{3,2,1,0:T(8,128)(2,1)S(1)}, u32[]{:S(2)}, u32[]{:S(2)}) async-start(bf16[4,8,16,512]{3,2,1,0:T(8,128)(2,1)} %get-tuple-element.76), calls=%async_computation.2 | async-start | bytes 1048576 | tf_op jit(solution)/shard_map/all_to_all | solution.py:48
  28.7 1.9 %gather_fusion.1 = s32[256]{0:T(256)S(1)} fusion(s32[256]{0:T(256)S(1)} %get-tuple-element.72, s32[1024]{0:T(1024)S(1)} %pad_clamp_fusion.2), kind=kCustom, calls=%fused_computation.5 | custom fusion | bytes 3072 | tf_op jit(solution)/shard_map/gather | solution.py:255
  31.3 3.8 %collective-permute-start.2 = (s32[1,64]{1,0:T(1,128)}, s32[1,64]{1,0:T(1,128)}, u32[]{:S(2)}, u32[]{:S(2)}) collective-permute-start(s32[1,64]{1,0:T(1,128)} %get-tuple-element.69), channel_id=1, source_target_pairs={{0,12},{4,8},{8,4},{12,0},{1,13},{5,9},{9,5},{13,1},{2,14},{6,10},... | collective-permute-start | bytes 776 | tf_op jit(solution)/shard_map/ppermute | solution.py:29
  36.2 5.8 %all-to-all-done.2 = bf16[4,8,16,512]{3,2,1,0:T(8,128)(2,1)S(1)} async-done(((bf16[4,8,16,512]{3,2,1,0:T(8,128)(2,1)}), bf16[4,8,16,512]{3,2,1,0:T(8,128)(2,1)S(1)}, u32[]{:S(2)}, u32[]{:S(2)}) %all-to-all-start.2) | async-done | bytes 524320 | tf_op jit(solution)/shard_map/all_to_all | solution.py:48
  42.0 3.6 %all-to-all-start.1 = ((bf16[4,8,16,512]{3,2,1,0:T(8,128)(2,1)}), bf16[4,8,16,512]{3,2,1,0:T(8,128)(2,1)S(1)}, u32[]{:S(2)}, u32[]{:S(2)}) async-start(bf16[4,8,16,512]{3,2,1,0:T(8,128)(2,1)} %get-tuple-element.77), calls=%async_computation.1 | async-start | bytes 1048576 | tf_op jit(solution)/shard_map/all_to_all | solution.py:47
  45.7 0.8 copy.154
  46.4 0.8 copy.153
  49.0 10.3 %all-to-all-done.1 = bf16[4,8,16,512]{3,2,1,0:T(8,128)(2,1)S(1)} async-done(((bf16[4,8,16,512]{3,2,1,0:T(8,128)(2,1)}), bf16[4,8,16,512]{3,2,1,0:T(8,128)(2,1)S(1)}, u32[]{:S(2)}, u32[]{:S(2)}) %all-to-all-start.1) | async-done | bytes 524320 | tf_op jit(solution)/shard_map/all_to_all | solution.py:47
  62.1 4.4 %all_gather.11 = f32[2,256,8]{1,2,0:T(8,128)S(1)} all-gather(f32[1,256,8]{1,2,0:T(8,128)S(1)} %maximum_bitcast_fusion.1), channel_id=1, replica_groups=mesh['scene'=2,'pts'=4,'view'=2,'head'=2] {'view'}, dimensions={0}, use_global_device_ids=true | all-gather | bytes 24576 | tf_op jit(solution)/shard_map/all_gather | solution.py:35
  66.5 4.5 %all_gather.9 = f32[2,256,8]{1,2,0:T(8,128)} all-gather(f32[1,256,8]{1,2,0:T(8,128)S(1)} %maximum_bitcast_fusion), channel_id=1, replica_groups=mesh['scene'=2,'pts'=4,'view'=2,'head'=2] {'view'}, dimensions={0}, use_global_device_ids=true | all-gather | bytes 24576 | tf_op jit(solution)/shard_map/all_gather | solution.py:35
  71.1 0.7 copy-done.12
  71.8 1.0 convolution_bitcast_fusion
  74.1 1.0 convolution_bitcast_fusion.1
  75.5 1.0 copy.116
  77.9 1.0 copy.139
  79.3 1.0 copy.138
  80.3 1.3 pad_maximum_fusion.1
  81.6 1.1 reshape.404
  82.7 2.6 %convolution_convert_fusion = bf16[32,8192]{1,0:T(8,128)(2,1)} fusion(f32[32,8192]{1,0:T(8,128)} %reshape.404, s32[32]{0:T(128)} %copy-done.26), kind=kOutput, calls=%fused_computation.10 | convolution fusion | flops 100926464 | bytes 1572992 | tf_op jit(solution)/shard_map/dot_general | solution.py:217
  85.4 3.5 %all-to-all-start.5 = ((bf16[4,8,16,512]{3,1,2,0:T(8,128)(2,1)}), bf16[4,8,16,512]{3,1,2,0:T(8,128)(2,1)S(1)}, u32[]{:S(2)}, u32[]{:S(2)}) async-start(bf16[4,8,16,512]{3,1,2,0:T(8,128)(2,1)} %bitcast.83), calls=%async_computation.5 | async-start | bytes 1048576 | tf_op jit(solution)/shard_map/all_to_all | solution.py:224
  90.2 0.8 gather_fusion.2
  91.1 1.6 %scatter_custom_fusion.1 = s32[256]{0:T(256)S(1)} fusion(s32[256]{0:T(256)S(1)} %bitcast.285, s32[256]{0:T(256)S(1)} %iota.31, s32[]{:T(128)} %constant.110.clone.1), kind=kCustom, calls=%fused_computation.153 | custom fusion | bytes 1028 | tf_op jit(solution)/shard_map/scatter | solution.py:260
  93.9 0.8 broadcast_in_dim.54
  94.8 1.2 copy.119
  96.1 0.8 broadcast_in_dim.53
  96.9 2.1 %copy.118 = f32[256,512]{1,0:T(8,128)} copy(f32[256,512]{0,1:T(8,128)} %bitcast.251) | data formatting | bytes 1048576 | tf_op jit(solution)/shard_map/while/body/eval_jaxpr/reshape | solution.py:65
  99.0 0.8 broadcast_in_dim.52
  99.8 2.0 %copy.117 = f32[256,512]{1,0:T(8,128)} copy(f32[256,512]{0,1:T(8,128)} %bitcast.252) | data formatting | bytes 1048576 | tf_op jit(solution)/shard_map/while/body/eval_jaxpr/reshape | solution.py:65
  102.7 0.7 copy.142
  103.7 2.6 %convert_multiply_fusion = (f32[256,512]{1,0:T(8,128)}, bf16[256,512]{1,0:T(8,128)(2,1)S(1)}) fusion(bf16[256,512]{1,0:T(8,128)(2,1)S(1)} %copy-done.9, f32[256,512]{1,0:T(8,128)S(1)} %copy.119, f32[256,512]{1,0:T(8,128)} %copy.118, f32[2,256,512]{2,1,0:T(8,128)} %all-gather.2.cloned.1.call-done, f32[256,512]{1,0:T(8,128)} %copy.117), kind=kLoop, calls=%fused_computation.57 | loop fusion | flops 1048576 | bytes 3670016 | tf_op jit(solution)/shard_map/mul | solution.py:159
  106.3 1.2 copy.126
  107.7 0.8 copy-done.13
  110.7 2.0 %gather_fusion = bf16[256,512]{1,0:T(8,128)(2,1)} fusion(bf16[256,512]{1,0:T(8,128)(2,1)S(1)} %get-tuple-element.48, s32[1024]{0:T(1024)} %copy-done.25), kind=kCustom, calls=%fused_computation.4 | custom fusion | bytes 525312 | tf_op jit(solution)/shard_map/gather | solution.py:254
  112.7 5.0 %all-to-all-start.3 = ((bf16[4,64,512]{2,1,0:T(8,128)(2,1)}), bf16[4,64,512]{2,1,0:T(8,128)(2,1)S(1)}, u32[]{:S(2)}, u32[]{:S(2)}) async-start(bf16[4,64,512]{2,1,0:T(8,128)(2,1)} %bitcast.39), calls=%async_computation.3 | async-start | bytes 524288 | tf_op jit(solution)/shard_map/all_to_all | solution.py:257
  118.0 0.9 copy-done.11
  121.5 1.4 convolution_convert_fusion.1
  122.9 1.6 %all-to-all-done.3 = bf16[4,64,512]{2,1,0:T(8,128)(2,1)S(1)} async-done(((bf16[4,64,512]{2,1,0:T(8,128)(2,1)}), bf16[4,64,512]{2,1,0:T(8,128)(2,1)S(1)}, u32[]{:S(2)}, u32[]{:S(2)}) %all-to-all-start.3) | async-done | bytes 262176 | tf_op jit(solution)/shard_map/all_to_all | solution.py:257
  124.5 3.5 %all-to-all-start.4 = ((bf16[4,8,16,512]{3,1,2,0:T(8,128)(2,1)}), bf16[4,8,16,512]{3,1,2,0:T(8,128)(2,1)S(1)}, u32[]{:S(2)}, u32[]{:S(2)}) async-start(bf16[4,8,16,512]{3,1,2,0:T(8,128)(2,1)} %bitcast.76), calls=%async_computation.4 | async-start | bytes 1048576 | tf_op jit(solution)/shard_map/all_to_all | solution.py:223
  128.5 15.9 %all-reduce.1 = bf16[256,512]{0,1:T(8,128)(2,1)S(1)} all-reduce(f32[256,512]{0,1:T(8,128)S(1)} %pad_maximum_fusion.3), channel_id=1, replica_groups=mesh['scene'=2,'pts'=4,'view'=2,'head'=2] {'view'}, use_global_device_ids=true, to_apply=%region_14.17 | all-reduce | flops 131072 | bytes 786432 | tf_op jit(solution)/shard_map/psum | solution.py:212
  144.4 0.8 copy.140
  145.2 2.0 %gather_fusion.3 = bf16[256,512]{1,0:T(8,128)(2,1)} fusion(bf16[256,512]{1,0:T(8,128)(2,1)S(1)} %bitcast.234, s32[1024]{0:T(1024)} %pad_clamp_fusion), kind=kCustom, calls=%fused_computation.7 | custom fusion | bytes 525312 | tf_op jit(solution)/shard_map/gather | solution.py:261
  147.4 0.7 copy.141
  (178 shorter events, 23.8 us)
Async XLA Ops:
  7.2 15.3 %copy-start = (bf16[8,16,512]{2,1,0:T(8,128)(2,1)S(1)}, bf16[8,16,512]{2,1,0:T(8,128)(2,1)}, u32[]{:S(2)}) copy-start(bf16[8,16,512]{2,1,0:T(8,128)(2,1)} %param.12) | copy-start | bytes 393220
  8.6 27.2 %copy-start.26 = (s32[32]{0:T(128)}, s32[32]{0:T(128)S(1)}, u32[]{:S(2)}) copy-start(s32[32]{0:T(128)S(1)} %get-tuple-element.43) | copy-start | bytes 388
  9.2 6.5 %copy-start.38 = (s32[256]{0:T(256)S(1)}, s32[256]{0:T(256)}, u32[]{:S(2)}) copy-start(s32[256]{0:T(256)} %param.14) | copy-start | bytes 3076
  9.2 11.9 %all-to-all-start = ((s32[4,1,8]{2,1,0:T(1,128)}), s32[4,1,8]{2,1,0:T(1,128)S(1)}, u32[]{:S(2)}, u32[]{:S(2)}) async-start(s32[4,1,8]{2,1,0:T(1,128)} %bitcast), calls=%async_computation | async-start | bytes 4096 | tf_op jit(solution)/shard_map/all_to_all | solution.py:43
  22.5 0.9 copy-start.3
  25.1 16.8 %all-to-all-start.2 = ((bf16[4,8,16,512]{3,2,1,0:T(8,128)(2,1)}), bf16[4,8,16,512]{3,2,1,0:T(8,128)(2,1)S(1)}, u32[]{:S(2)}, u32[]{:S(2)}) async-start(bf16[4,8,16,512]{3,2,1,0:T(8,128)(2,1)} %get-tuple-element.76), calls=%async_computation.2 | async-start | bytes 1048576 | tf_op jit(solution)/shard_map/all_to_all | solution.py:48
  28.7 2.0 %copy-start.25 = (s32[1024]{0:T(1024)}, s32[1024]{0:T(1024)S(1)}, u32[]{:S(2)}) copy-start(s32[1024]{0:T(1024)S(1)} %pad_clamp_fusion.2) | copy-start | bytes 12292
  28.7 7.2 %copy-start.14 = (bf16[256,512]{1,0:T(8,128)(2,1)S(1)}, bf16[256,512]{1,0:T(8,128)(2,1)}, u32[]{:S(2)}) copy-start(bf16[256,512]{1,0:T(8,128)(2,1)} %param.10) | copy-start | bytes 786436
  31.3 57.5 %collective-permute-start.2 = (s32[1,64]{1,0:T(1,128)}, s32[1,64]{1,0:T(1,128)}, u32[]{:S(2)}, u32[]{:S(2)}) collective-permute-start(s32[1,64]{1,0:T(1,128)} %get-tuple-element.69), channel_id=1, source_target_pairs={{0,12},{4,8},{8,4},{12,0},{1,13},{5,9},{9,5},{13,1},{2,14},{6,10},... | collective-permute-start | bytes 776 | tf_op jit(solution)/shard_map/ppermute | solution.py:29
  35.1 53.8 %collective-permute-start.1 = (s32[1,64]{1,0:T(1,128)}, s32[1,64]{1,0:T(1,128)}, u32[]{:S(2)}, u32[]{:S(2)}) collective-permute-start(s32[1,64]{1,0:T(1,128)} %get-tuple-element.70), channel_id=1, source_target_pairs={{0,8},{4,12},{8,0},{12,4},{1,9},{5,13},{9,1},{13,5},{2,10},{6,14},... | collective-permute-start | bytes 776 | tf_op jit(solution)/shard_map/ppermute | solution.py:29
  35.1 53.8 %collective-permute-start = (s32[1,64]{1,0:T(1,128)}, s32[1,64]{1,0:T(1,128)}, u32[]{:S(2)}, u32[]{:S(2)}) collective-permute-start(s32[1,64]{1,0:T(1,128)} %get-tuple-element.71), channel_id=1, source_target_pairs={{0,4},{4,0},{8,12},{12,8},{1,5},{5,1},{9,13},{13,9},{2,6},{6,2},{1... | collective-permute-start | bytes 776 | tf_op jit(solution)/shard_map/ppermute | solution.py:29
  36.0 24.4 %copy-start.6 = (bf16[2,128,256]{1,2,0:T(8,128)(2,1)}, bf16[2,128,256]{1,2,0:T(8,128)(2,1)S(1)}, u32[]{:S(2)}) copy-start(bf16[2,128,256]{1,2,0:T(8,128)(2,1)S(1)} %copy.152) | copy-start | bytes 393220
  36.2 25.4 %copy-start.4 = (bf16[2,128,256]{1,2,0:T(8,128)(2,1)}, bf16[2,128,256]{1,2,0:T(8,128)(2,1)S(1)}, u32[]{:S(2)}) copy-start(bf16[2,128,256]{1,2,0:T(8,128)(2,1)S(1)} %copy.151) | copy-start | bytes 393220
  42.0 3.7 %copy-start.8 = (bf16[256,512]{1,0:T(8,128)(2,1)S(1)}, bf16[256,512]{1,0:T(8,128)(2,1)}, u32[]{:S(2)}) copy-start(bf16[256,512]{1,0:T(8,128)(2,1)} %param.15) | copy-start | bytes 786436
  42.0 17.4 %all-to-all-start.1 = ((bf16[4,8,16,512]{3,2,1,0:T(8,128)(2,1)}), bf16[4,8,16,512]{3,2,1,0:T(8,128)(2,1)S(1)}, u32[]{:S(2)}, u32[]{:S(2)}) async-start(bf16[4,8,16,512]{3,2,1,0:T(8,128)(2,1)} %get-tuple-element.77), calls=%async_computation.1 | async-start | bytes 1048576 | tf_op jit(solution)/shard_map/all_to_all | solution.py:47
  45.6 57.9 %all-gather.2.cloned.1.call-start = ((), (), s32[]{:S(2)}) async-start(), calls=%async_computation.6 | async-start | bytes 1572864 | tf_op jit(solution)/shard_map/all_gather | solution.py:35
  60.3 0.7 copy-start.1
  61.4 5.1 %copy-start.22 = (f32[2,4,128]{2,1,0:T(4,128)}, f32[2,4,128]{2,1,0:T(4,128)S(1)}, u32[]{:S(2)}) copy-start(f32[2,4,128]{2,1,0:T(4,128)S(1)} %get-tuple-element.80) | copy-start | bytes 12292
  61.9 4.6 %copy-start.21 = (f32[2,4,128]{2,1,0:T(4,128)}, f32[2,4,128]{2,1,0:T(4,128)S(1)}, u32[]{:S(2)}) copy-start(f32[2,4,128]{2,1,0:T(4,128)S(1)} %get-tuple-element.82) | copy-start | bytes 12292
  71.1 0.7 copy-start.12
  73.4 0.7 copy-start.10
  76.6 0.7 copy-start.15
  76.6 0.9 copy-start.19
  77.3 0.6 copy-start.33
  77.3 0.6 copy-start.35
  77.3 1.6 %copy-start.29 = (f32[2,4,128]{2,1,0:T(4,128)}, f32[2,4,128]{2,1,0:T(4,128)S(1)}, u32[]{:S(2)}) copy-start(f32[2,4,128]{2,1,0:T(4,128)S(1)} %get-tuple-element.62) | copy-start | bytes 12292
  77.3 1.6 %copy-start.31 = (f32[2,4,128]{2,1,0:T(4,128)}, f32[2,4,128]{2,1,0:T(4,128)S(1)}, u32[]{:S(2)}) copy-start(f32[2,4,128]{2,1,0:T(4,128)S(1)} %get-tuple-element.85) | copy-start | bytes 12292
  77.9 1.0 copy-start.17
  85.4 16.5 %all-to-all-start.5 = ((bf16[4,8,16,512]{3,1,2,0:T(8,128)(2,1)}), bf16[4,8,16,512]{3,1,2,0:T(8,128)(2,1)S(1)}, u32[]{:S(2)}, u32[]{:S(2)}) async-start(bf16[4,8,16,512]{3,1,2,0:T(8,128)(2,1)} %bitcast.83), calls=%async_computation.5 | async-start | bytes 1048576 | tf_op jit(solution)/shard_map/all_to_all | solution.py:224
  88.9 0.7 copy-start.37
  90.2 3.1 %copy-start.16 = (f32[2,256,8]{1,2,0:T(8,128)S(1)}, f32[2,256,8]{1,2,0:T(8,128)}, u32[]{:S(2)}) copy-start(f32[2,256,8]{1,2,0:T(8,128)} %all_gather.9) | copy-start | bytes 49156
  94.8 1.3 copy-start.24
  96.9 2.1 %copy-start.23 = (f32[256,8]{0,1:T(8,128)S(1)}, f32[256,8]{0,1:T(8,128)}, u32[]{:S(2)}) copy-start(f32[256,8]{0,1:T(8,128)} %get-tuple-element.50) | copy-start | bytes 24580
  101.8 0.7 copy-start.28
  102.7 1.0 copy-start.9
  107.6 1.0 copy-start.13
  107.6 1.0 copy-start.20
  107.6 0.9 copy-start.34
  107.7 0.9 copy-start.36
  108.6 1.0 copy-start.2
  109.5 0.9 copy-start.7
  112.7 11.8 %all-to-all-start.3 = ((bf16[4,64,512]{2,1,0:T(8,128)(2,1)}), bf16[4,64,512]{2,1,0:T(8,128)(2,1)S(1)}, u32[]{:S(2)}, u32[]{:S(2)}) async-start(bf16[4,64,512]{2,1,0:T(8,128)(2,1)} %bitcast.39), calls=%async_computation.3 | async-start | bytes 524288 | tf_op jit(solution)/shard_map/all_to_all | solution.py:257
  118.0 1.0 copy-start.11
  118.0 1.0 copy-start.18
  118.0 1.0 copy-start.30
  118.0 1.0 copy-start.32
  119.4 0.9 copy-start.5
  124.5 22.7 %all-to-all-start.4 = ((bf16[4,8,16,512]{3,1,2,0:T(8,128)(2,1)}), bf16[4,8,16,512]{3,1,2,0:T(8,128)(2,1)S(1)}, u32[]{:S(2)}, u32[]{:S(2)}) async-start(bf16[4,8,16,512]{3,1,2,0:T(8,128)(2,1)} %bitcast.76), calls=%async_computation.4 | async-start | bytes 1048576 | tf_op jit(solution)/shard_map/all_to_all | solution.py:223
  (1 other events, 0.6 us)
Sparse Core Ops, SparseCore 0:
  76.7 20.4 all-gather.1
